TPU v7x, 32 devices: a whole 2x2x4 slice. The times are simulated.
32 devices in a mesh: groups: 2 (over y), ax: 4 (over z), az: 2 (over x), rad: 2 (over core).
Axes of the slice: x: 2, y: 2, z: 4, core: 2. Of those that a mesh axis runs over, the one named last changes fastest.
Arguments:
- flow_state: float32 [4, 16, 96, 256], P(None, ('groups', 'ax'), 'rad', 'az'), parts along dimension 1, may hold values from -2 to 2, as said below
- cycle_widths: int32 [8], replicated, may hold values from 2 to 256, as said below
Outputs:
- advanced: float32 [4, 16, 96, 256], P(None, ('groups', 'ax'), 'rad', 'az'), parts along dimension 1
There are 2 independent parts, one for each index of `groups`. A program takes and returns all parts, laid end to end along the dimension named above; an argument that names none is the same for every part. Nothing has to cross between parts.
Inputs may be any that keep to these rules, and one draw needn't show every extreme that they name: `flow_state`: channel 0 lies in 0 to 1. `cycle_widths`: each entry is a power of two that divides 256; entry 0 equals 256.
All inputs are finite; a program needn't handle non-finite values.
Results may differ from a plain program's by a relative error of at most 0.0003.
Values sent between devices are 32-bit elements; how exact they have to be, the bound alone decides.
A program may use at most 64 MiB of HBM per device.

v0:
```python
import math

import jax
import jax.numpy as jnp
from jax import lax
from jax.sharding import PartitionSpec as P

STEPS = 2


DT = 0.2
KAPPA = 0.05
VISC = 0.1
RHO_RATIO = 20.0


def extended_2(block, sides, width, periodic):
    for axis, dim in sides:
        count = lax.axis_size(axis)
        forward = [(i, i + 1) for i in range(count - 1)]
        if periodic:
            forward.append((count - 1, 0))
        backward = [(target, source) for source, target in forward]
        low = lax.ppermute(
            lax.slice_in_dim(block, block.shape[dim] - width, None, axis=dim), axis, forward
        )
        high = lax.ppermute(lax.slice_in_dim(block, 0, width, axis=dim), axis, backward)
        block = jnp.concatenate([low, block, high], axis=dim)
    return block


def rates(
    center,
    upper_plane,
    lower_plane,
    outer_cycle,
    inner_cycle,
    ahead_cell,
    behind_cell,
    radius,
    angle_step,
):
    level_set = center[0]
    axial_speed = center[1]
    radial_speed = center[2]
    swirl_speed = center[3]
    reciprocal = 1.0 / radius
    arc_scale = 1.0 / (2.0 * radius * angle_step)
    level_flux = (upper_plane[1] * upper_plane[0] - lower_plane[1] * lower_plane[0]) * 0.5
    level_flux = (
        level_flux
        + (
            (radius + 1.0) * outer_cycle[2] * outer_cycle[0]
            - (radius - 1.0) * inner_cycle[2] * inner_cycle[0]
        )
        * 0.5
        * reciprocal
    )
    level_flux = (
        level_flux + (ahead_cell[3] * ahead_cell[0] - behind_cell[3] * behind_cell[0]) * arc_scale
    )
    diffused = (
        upper_plane
        + lower_plane
        - 2.0 * center
        + ((radius + 0.5) * (outer_cycle - center) - (radius - 0.5) * (center - inner_cycle))
        * reciprocal
    )
    level_rate = -level_flux + KAPPA * diffused[0]
    density = 1.0 + (RHO_RATIO - 1.0) * jnp.clip(level_set, 0.0, 1.0)
    transport = axial_speed * (upper_plane[1:] - lower_plane[1:]) * 0.5
    transport = transport + radial_speed * (outer_cycle[1:] - inner_cycle[1:]) * 0.5
    transport = transport + swirl_speed * (ahead_cell[1:] - behind_cell[1:]) * arc_scale
    viscous = VISC / density * diffused[1:]
    curvature = jnp.stack(
        [
            jnp.zeros_like(level_set),
            swirl_speed * swirl_speed * reciprocal,
            -swirl_speed * radial_speed * reciprocal,
        ]
    )
    velocity_rates = -transport + viscous + curvature
    return DT * jnp.concatenate([level_rate[None], velocity_rates], 0)


def local(flow_state, cycle_widths):
    sectors = lax.axis_size("az")
    radial_rows = flow_state.shape[2]
    columns = flow_state.shape[3]
    cycle_count = cycle_widths.shape[0]
    rad_place = lax.axis_index("rad")
    az_place = lax.axis_index("az")
    angle_step = 2.0 * math.pi / (sectors * columns)
    radius = (
        (rad_place * radial_rows + jnp.arange(radial_rows, dtype=jnp.int32)).astype(jnp.float32)
        + 0.5
    )[:, None]
    mirror = jnp.array([1.0, 1.0, -1.0, -1.0], jnp.float32)[:, None, None]
    cycle_column = cycle_widths[:, None]
    cycle_divisor = cycle_column.astype(jnp.float32)
    result = flow_state
    for repeat in range(STEPS):
        extended = extended_2(result, (("ax", 1),), 1, False)
        middle = extended[:, 1:-1]
        side_rims = extended_2(middle, (("az", 3),), 1, True)
        radial = extended_2(middle, (("rad", 2),), 1, False)
        innermost = middle[:, :, 0, :]
        full_cycle = lax.all_gather(innermost, "az", axis=2, tiled=True)
        partner = (az_place + sectors // 2) % sectors
        opposite = lax.dynamic_slice_in_dim(full_cycle, partner * columns, columns, 2)
        opposite = opposite * mirror
        inner_rows = radial[:, :, :-2]
        first_row = jnp.where(rad_place == 0, opposite, inner_rows[:, :, 0])
        inner_rows = jnp.concatenate([first_row[:, :, None], inner_rows[:, :, 1:]], 2)
        increment = rates(
            middle,
            extended[:, 2:],
            extended[:, :-2],
            radial[:, :, 2:],
            inner_rows,
            side_rims[..., 2:],
            side_rims[..., :-2],
            radius,
            angle_step,
        )
        cycle_head = increment[:, :, :cycle_count]
        index_shape = cycle_head.shape
        leading = jnp.zeros(index_shape[:3] + (1,), jnp.float32)
        running = jnp.concatenate([leading, jnp.cumsum(cycle_head, axis=3)], 3)
        local_width = jnp.minimum(cycle_column, columns)
        local_column = jnp.arange(columns, dtype=jnp.int32)
        block_start = local_column[None, :] // local_width * local_width
        near_sum = jnp.take_along_axis(
            running, jnp.broadcast_to(block_start + local_width, index_shape), axis=3
        )
        near_sum = near_sum - jnp.take_along_axis(
            running, jnp.broadcast_to(block_start, index_shape), axis=3
        )
        sector_sum = running[..., columns]
        gathered = lax.all_gather(sector_sum[..., None], "az", axis=3, tiled=True)
        group_size = jnp.maximum(cycle_widths // columns, 1)[:, None]
        member = (
            jnp.arange(sectors, dtype=jnp.int32)[None, :] // group_size == az_place // group_size
        )
        far_sum = jnp.sum(gathered * member.astype(jnp.float32), axis=3)
        block_sum = jnp.where(cycle_column > columns, far_sum[..., None], near_sum)
        block_mean = block_sum / cycle_divisor
        cycle_head = jnp.where(rad_place == 0, block_mean, cycle_head)
        increment = jnp.concatenate([cycle_head, increment[:, :, cycle_count:]], 2)
        result = middle + increment
    return result


def solution(mesh):
    return jax.shard_map(
        local,
        mesh=mesh,
        in_specs=(P(None, ("groups", "ax"), "rad", "az"), P()),
        out_specs=P(None, ("groups", "ax"), "rad", "az"),
        check_vma=False,
    )
```

profile of v0, /device:TPU:0, one launch (start us, length us, event | category | flops | bytes accessed | tf_op | source)
XLA Modules:
  0.0 373.1 jit_solution(4338981845610379736)
XLA Ops:
  0.0 0.8 fusion.106
  0.8 2.4 collective-permute-start.3
  3.2 1.0 fusion.105
  4.2 4.3 %collective-permute-start.1 = (f32[4,1,48,128]{3,2,1,0:T(8,128)S(1)}, f32[4,1,48,128]{3,2,1,0:T(8,128)S(1)}, u32[]{:S(2)}, u32[]{:S(2)}) collective-permute-start(f32[4,1,48,128]{3,2,1,0:T(8,128)S(1)} %get-tuple-element.33), channel_id=1, source_target_pairs={{0,4},{4,8},{8,12},{1,5},{5,9},{9,13},{2,6},{6,10},{10,14},{3,7},{... | collective-permute-start | bytes 294920 | tf_op jit(solution)/shard_map/ppermute | solution.py:24
  8.5 1.3 collective-permute-start.2
  9.8 1.3 collective-permute-start
  11.1 0.1 fusion.104
  11.2 1.6 collective-permute-start.4
  12.8 6.2 %all-gather = f32[4,2,1,256]{3,2,1,0:T(1,128)S(1)} all-gather(f32[4,2,1,128]{3,2,1,0:T(1,128)S(1)} %get-tuple-element.37), channel_id=2, replica_groups=mesh['groups'=2,'ax'=4,'az'=2,'rad'=2] {'az'}, dimensions={3}, use_global_device_ids=true | all-gather | bytes 12288 | tf_op jit(solution)/shard_map/all_gather | solution.py:108
  19.1 0.1 and_select_fusion.1
  19.2 0.2 broadcast_add_fusion.2
  19.4 0.2 broadcast_compare_fusion.1
  19.7 0.1 multiply_multiply_fusion.3
  19.8 0.1 compare_convert_fusion
  19.9 1.6 collective-permute-start.5
  21.7 0.1 constant_dynamic-update-slice_fusion.6
  21.9 5.0 %collective-permute-done.5 = f32[4,2,48,1]{3,2,1,0:T(8,128)S(1)} collective-permute-done((f32[4,2,48,1]{3,2,1,0:T(8,128)S(1)}, f32[4,2,48,1]{3,2,1,0:T(8,128)S(1)}, u32[]{:S(2)}, u32[]{:S(2)}) %collective-permute-start.5) | collective-permute-done | bytes 1568 | tf_op jit(solution)/shard_map/ppermute | solution.py:24
  26.9 0.1 fusion.66
  27.1 0.2 fusion.36
  27.3 2.3 reduce_window_sum.17
  29.6 0.1 concatenate.69
  29.8 76.3 %gather_fusion = f32[8192]{0:T(1024)S(1)} fusion(f32[4,2,8,129]{3,2,1,0:T(8,128)S(1)} %concatenate.69, s32[8192]{0:T(1024)S(1)} %bitcast.62), kind=kCustom, calls=%fused_computation.clone | custom fusion | bytes 196608 | tf_op jit(solution)/shard_map/jit(take_along_axis)/gather | solution.py:133
  106.1 76.3 %gather_fusion.1 = f32[8192]{0:T(1024)S(1)} fusion(f32[4,2,8,129]{3,2,1,0:T(8,128)S(1)} %concatenate.69, s32[8192]{0:T(1024)S(1)} %bitcast.60), kind=kCustom, calls=%fused_computation.1.clone | custom fusion | bytes 196608 | tf_op jit(solution)/shard_map/jit(take_along_axis)/gather | solution.py:136
  182.4 0.1 copy.17
  182.5 4.3 %all_gather.13 = f32[4,2,8,2]{2,0,1,3:T(4,128)S(1)} all-gather(f32[4,2,8,1]{2,0,1,3:T(4,128)S(1)} %copy.17), channel_id=1, replica_groups=mesh['groups'=2,'ax'=4,'az'=2,'rad'=2] {'az'}, dimensions={3}, use_global_device_ids=true | all-gather | bytes 768 | tf_op jit(solution)/shard_map/all_gather | solution.py:140
  186.8 0.1 fusion.91
  187.0 4.3 %all-gather.1 = f32[4,2,1,256]{3,2,1,0:T(1,128)S(1)} all-gather(f32[4,2,1,128]{3,2,1,0:T(1,128)S(1)} %get-tuple-element.22), channel_id=3, replica_groups=mesh['groups'=2,'ax'=4,'az'=2,'rad'=2] {'az'}, dimensions={3}, use_global_device_ids=true | all-gather | bytes 12288 | tf_op jit(solution)/shard_map/all_gather | solution.py:108
  191.3 1.3 collective-permute-start.8
  192.6 0.1 fusion.101
  192.7 0.1 multiply_multiply_fusion.1
  192.8 1.3 collective-permute-start.6
  194.1 5.1 %collective-permute-start.7 = (f32[4,1,48,128]{3,2,1,0:T(8,128)S(1)}, f32[4,1,48,128]{3,2,1,0:T(8,128)S(1)}, u32[]{:S(2)}, u32[]{:S(2)}) collective-permute-start(f32[4,1,48,128]{3,2,1,0:T(8,128)S(1)} %get-tuple-element.21), channel_id=1, source_target_pairs={{0,4},{4,8},{8,12},{1,5},{5,9},{9,13},{2,6},{6,10},{10,14},{3,7},{... | collective-permute-start | bytes 294920 | tf_op jit(solution)/shard_map/ppermute | solution.py:24
  199.1 2.7 collective-permute-start.9
  201.9 1.6 collective-permute-start.10
  203.5 0.7 collective-permute-start.11
  204.3 0.1 fusion.5
  204.4 5.4 %collective-permute-done.10 = f32[4,2,48,1]{3,2,1,0:T(8,128)S(1)} collective-permute-done((f32[4,2,48,1]{3,2,1,0:T(8,128)S(1)}, f32[4,2,48,1]{3,2,1,0:T(8,128)S(1)}, u32[]{:S(2)}, u32[]{:S(2)}) %collective-permute-start.10) | collective-permute-done | bytes 1568 | tf_op jit(solution)/shard_map/ppermute | solution.py:27
  209.8 2.6 collective-permute-done.11
  212.4 0.2 fusion.56
  212.6 0.2 fusion.27
  212.8 2.3 reduce_window_sum.18
  215.1 0.1 concatenate.78
  215.2 76.3 %gather_fusion.2 = f32[8192]{0:T(1024)S(1)} fusion(f32[4,2,8,129]{3,2,1,0:T(8,128)S(1)} %concatenate.78, s32[8192]{0:T(1024)S(1)} %bitcast.63), kind=kCustom, calls=%fused_computation.2.clone | custom fusion | bytes 196608 | tf_op jit(solution)/shard_map/jit(take_along_axis)/gather | solution.py:133
  291.5 76.3 %gather_fusion.3 = f32[8192]{0:T(1024)S(1)} fusion(f32[4,2,8,129]{3,2,1,0:T(8,128)S(1)} %concatenate.78, s32[8192]{0:T(1024)S(1)} %bitcast.61), kind=kCustom, calls=%fused_computation.3.clone | custom fusion | bytes 196608 | tf_op jit(solution)/shard_map/jit(take_along_axis)/gather | solution.py:136
  367.9 0.1 copy.20
  368.0 4.3 %all_gather.15 = f32[4,2,8,2]{2,0,1,3:T(4,128)S(1)} all-gather(f32[4,2,8,1]{2,0,1,3:T(4,128)S(1)} %copy.20), channel_id=1, replica_groups=mesh['groups'=2,'ax'=4,'az'=2,'rad'=2] {'az'}, dimensions={3}, use_global_device_ids=true | all-gather | bytes 768 | tf_op jit(solution)/shard_map/all_gather | solution.py:140
  372.3 0.1 fusion.88
  372.4 0.7 maximum_add_fusion.1
  (50 shorter events, 0.7 us)
Async XLA Ops:
  0.0 11.1 %copy-start = (f32[4,2,48,128]{3,2,1,0:T(8,128)S(1)}, f32[4,2,48,128]{3,2,1,0:T(8,128)}, u32[]{:S(2)}) copy-start(f32[4,2,48,128]{3,2,1,0:T(8,128)} %param.9) | copy-start | bytes 589828
  0.8 19.1 %collective-permute-start.3 = (f32[4,2,1,128]{3,1,0,2:T(2,128)S(1)}, f32[4,2,1,128]{3,1,0,2:T(2,128)S(1)}, u32[]{:S(2)}, u32[]{:S(2)}) collective-permute-start(f32[4,2,1,128]{3,1,0,2:T(2,128)S(1)} %bitcast.82), channel_id=1, source_target_pairs={{0,1},{2,3},{4,5},{6,7},{8,9},{10,11},{12,13},{14,15},{16,17},{18,... | collective-permute-start | bytes 12296 | tf_op jit(solution)/shard_map/ppermute | solution.py:24
  4.2 17.4 %collective-permute-start.1 = (f32[4,1,48,128]{3,2,1,0:T(8,128)S(1)}, f32[4,1,48,128]{3,2,1,0:T(8,128)S(1)}, u32[]{:S(2)}, u32[]{:S(2)}) collective-permute-start(f32[4,1,48,128]{3,2,1,0:T(8,128)S(1)} %get-tuple-element.33), channel_id=1, source_target_pairs={{0,4},{4,8},{8,12},{1,5},{5,9},{9,13},{2,6},{6,10},{10,14},{3,7},{... | collective-permute-start | bytes 294920 | tf_op jit(solution)/shard_map/ppermute | solution.py:24
  8.5 13.2 %collective-permute-start.2 = (f32[4,2,1,128]{3,2,1,0:T(1,128)S(1)}, f32[4,2,1,128]{3,2,1,0:T(1,128)S(1)}, u32[]{:S(2)}, u32[]{:S(2)}) collective-permute-start(f32[4,2,1,128]{3,2,1,0:T(1,128)S(1)} %get-tuple-element.37), channel_id=1, source_target_pairs={{1,0},{3,2},{5,4},{7,6},{9,8},{11,10},{13,12},{15,14},{17,16},{19,... | collective-permute-start | bytes 12296 | tf_op jit(solution)/shard_map/ppermute | solution.py:27
  9.8 9.3 %copy-start.2 = (s32[8]{0:T(128)S(1)}, s32[8]{0:T(128)}, u32[]{:S(2)}) copy-start(s32[8]{0:T(128)} %param.10) | copy-start | bytes 100
  9.8 11.8 %collective-permute-start = (f32[4,1,48,128]{3,2,1,0:T(8,128)S(1)}, f32[4,1,48,128]{3,2,1,0:T(8,128)S(1)}, u32[]{:S(2)}, u32[]{:S(2)}) collective-permute-start(f32[4,1,48,128]{3,2,1,0:T(8,128)S(1)} %get-tuple-element.32), channel_id=1, source_target_pairs={{4,0},{8,4},{12,8},{5,1},{9,5},{13,9},{6,2},{10,6},{14,10},{7,3},{... | collective-permute-start | bytes 294920 | tf_op jit(solution)/shard_map/ppermute | solution.py:27
  11.2 10.3 %copy-start.1 = (f32[4]{0:T(128)S(1)}, f32[4]{0:T(128)}, u32[]{:S(2)}) copy-start(f32[4]{0:T(128)} %constant.114.clone) | copy-start | bytes 52
  11.2 10.6 %collective-permute-start.4 = (f32[4,2,48,1]{3,2,1,0:T(8,128)S(1)}, f32[4,2,48,1]{3,2,1,0:T(8,128)S(1)}, u32[]{:S(2)}, u32[]{:S(2)}) collective-permute-start(f32[4,2,48,1]{3,2,1,0:T(8,128)S(1)} %get-tuple-element.28), channel_id=1, source_target_pairs={{2,0},{0,2},{3,1},{1,3},{6,4},{4,6},{7,5},{5,7},{10,8},{8,10},{11,... | collective-permute-start | bytes 4616 | tf_op jit(solution)/shard_map/ppermute | solution.py:27
  19.9 7.0 %collective-permute-start.5 = (f32[4,2,48,1]{3,2,1,0:T(8,128)S(1)}, f32[4,2,48,1]{3,2,1,0:T(8,128)S(1)}, u32[]{:S(2)}, u32[]{:S(2)}) collective-permute-start(f32[4,2,48,1]{3,2,1,0:T(8,128)S(1)} %get-tuple-element.29), channel_id=1, source_target_pairs={{0,2},{2,0},{1,3},{3,1},{4,6},{6,4},{5,7},{7,5},{8,10},{10,8},{9,1... | collective-permute-start | bytes 4616 | tf_op jit(solution)/shard_map/ppermute | solution.py:24
  191.3 13.0 %collective-permute-start.8 = (f32[4,2,1,128]{3,2,1,0:T(1,128)S(1)}, f32[4,2,1,128]{3,2,1,0:T(1,128)S(1)}, u32[]{:S(2)}, u32[]{:S(2)}) collective-permute-start(f32[4,2,1,128]{3,2,1,0:T(1,128)S(1)} %get-tuple-element.22), channel_id=1, source_target_pairs={{1,0},{3,2},{5,4},{7,6},{9,8},{11,10},{13,12},{15,14},{17,16},{19,... | collective-permute-start | bytes 12296 | tf_op jit(solution)/shard_map/ppermute | solution.py:27
  192.8 11.5 %collective-permute-start.6 = (f32[4,1,48,128]{3,2,1,0:T(8,128)S(1)}, f32[4,1,48,128]{3,2,1,0:T(8,128)S(1)}, u32[]{:S(2)}, u32[]{:S(2)}) collective-permute-start(f32[4,1,48,128]{3,2,1,0:T(8,128)S(1)} %get-tuple-element.20), channel_id=1, source_target_pairs={{4,0},{8,4},{12,8},{5,1},{9,5},{13,9},{6,2},{10,6},{14,10},{7,3},{... | collective-permute-start | bytes 294920 | tf_op jit(solution)/shard_map/ppermute | solution.py:27
  194.1 10.2 %collective-permute-start.7 = (f32[4,1,48,128]{3,2,1,0:T(8,128)S(1)}, f32[4,1,48,128]{3,2,1,0:T(8,128)S(1)}, u32[]{:S(2)}, u32[]{:S(2)}) collective-permute-start(f32[4,1,48,128]{3,2,1,0:T(8,128)S(1)} %get-tuple-element.21), channel_id=1, source_target_pairs={{0,4},{4,8},{8,12},{1,5},{5,9},{9,13},{2,6},{6,10},{10,14},{3,7},{... | collective-permute-start | bytes 294920 | tf_op jit(solution)/shard_map/ppermute | solution.py:24
  199.1 4.3 %collective-permute-start.9 = (f32[4,2,1,128]{3,1,0,2:T(2,128)S(1)}, f32[4,2,1,128]{3,1,0,2:T(2,128)S(1)}, u32[]{:S(2)}, u32[]{:S(2)}) collective-permute-start(f32[4,2,1,128]{3,1,0,2:T(2,128)S(1)} %bitcast.83), channel_id=1, source_target_pairs={{0,1},{2,3},{4,5},{6,7},{8,9},{10,11},{12,13},{14,15},{16,17},{18,... | collective-permute-start | bytes 12296 | tf_op jit(solution)/shard_map/ppermute | solution.py:24
  201.9 7.9 %collective-permute-start.10 = (f32[4,2,48,1]{3,2,1,0:T(8,128)S(1)}, f32[4,2,48,1]{3,2,1,0:T(8,128)S(1)}, u32[]{:S(2)}, u32[]{:S(2)}) collective-permute-start(f32[4,2,48,1]{3,2,1,0:T(8,128)S(1)} %get-tuple-element.18), channel_id=1, source_target_pairs={{2,0},{0,2},{3,1},{1,3},{6,4},{4,6},{7,5},{5,7},{10,8},{8,10},{11,... | collective-permute-start | bytes 4616 | tf_op jit(solution)/shard_map/ppermute | solution.py:27
  203.5 8.9 %collective-permute-start.11 = (f32[4,2,48,1]{3,2,1,0:T(8,128)S(1)}, f32[4,2,48,1]{3,2,1,0:T(8,128)S(1)}, u32[]{:S(2)}, u32[]{:S(2)}) collective-permute-start(f32[4,2,48,1]{3,2,1,0:T(8,128)S(1)} %get-tuple-element.19), channel_id=1, source_target_pairs={{0,2},{2,0},{1,3},{3,1},{4,6},{6,4},{5,7},{7,5},{8,10},{10,8},{9,1... | collective-permute-start | bytes 4616 | tf_op jit(solution)/shard_map/ppermute | solution.py:24
where the time goes:
time: 373 us
  local copies, waits for them, and re-layouts  308 us (83%)
  starting transfers between devices  25 us (7%)
  blocking collectives  19.2 us (5%)
  waiting for transfers between devices  13 us (3%)
  other arithmetic  7.46 us (2%)
    gather x2, local copies, waits for them, and re-layouts, local(): jnp.take_along_axis(running, jnp.broadcast_to(block_start + local_width,...  153 us
    gather x2, local copies, waits for them, and re-layouts, local(): jnp.take_along_axis(running, jnp.broadcast_to(block_start, index_shape),...  153 us
    ppermute x6, starting transfers between devices, extended_2(): lax.ppermute(lax.slice_in_dim(block, block.shape[dim] - width, None, axis...  16.8 us
    all_gather x2, blocking collectives, local(): full_cycle = lax.all_gather(innermost, 'az', axis=2, tiled=True)  10.5 us
    all_gather x2, blocking collectives, local(): gathered = lax.all_gather(sector_sum[..., None], 'az', axis=3, tiled=True)  8.66 us
    ppermute x6, starting transfers between devices, extended_2(): lax.ppermute(lax.slice_in_dim(block, 0, width, axis=dim), axis, backward)  8.26 us
    ppermute x6, waiting for transfers between devices, extended_2(): lax.ppermute(lax.slice_in_dim(block, block.shape[dim] - width, None, axis...  7.62 us
  transfers between devices with their start and end apart: 12, of which 3 were waited for; matrix products, arithmetic and copies ran while one was open for 1% of the time, Pallas kernels for 0%

commit v1 on v0

v1 whole, which is shorter than its diff:
```python
import functools
import math

import jax
import jax.numpy as jnp
from jax import lax
from jax.experimental import pallas as pl
from jax.experimental.pallas import tpu as pltpu
from jax.sharding import PartitionSpec as P

STEPS = 2
DT = 0.2
KAPPA = 0.05
VISC = 0.1
RHO_RATIO = 20.0
PAD = 8
MESH = pl.DeviceIdType.MESH


def kernel(
    sizes,
    bounds,
    flow_ref,
    width_ref,
    out_ref,
    state,
    increment,
    spread,
    low_plane,
    high_plane,
    edge_out,
    edge_left,
    edge_right,
    row_out,
    row_in,
    sum_out,
    sum_in,
    load_sem,
    low_send,
    low_recv,
    high_send,
    high_recv,
    left_send,
    left_recv,
    right_send,
    right_recv,
    row_send,
    row_recv,
    opposite_send,
    opposite_recv,
    sum_send,
    sum_recv,
):
    axials, sectors, rads = sizes
    channels, planes, rows, columns = flow_ref.shape
    blocks = channels * planes
    rings = width_ref.shape[0]
    chunks = len(bounds) - 1
    ax = lax.axis_index("ax")
    az = lax.axis_index("az")
    rad = lax.axis_index("rad")
    angle_step = 2.0 * math.pi / (sectors * columns)
    half_arc = DT / (2.0 * angle_step)
    has_low = ax > 0
    has_high = ax < axials - 1
    has_inner = rad > 0
    has_outer = rad < rads - 1
    at_axis = rad == 0
    left = (az + sectors - 1) % sectors
    right = (az + 1) % sectors
    partner = (az + sectors // 2) % sectors

    load = pltpu.make_async_copy(
        flow_ref, state.at[0, :, :, pl.ds(PAD, rows)], load_sem
    )
    load.start()

    barrier = pltpu.get_barrier_semaphore()

    def greet(axis, place):
        pl.semaphore_signal(barrier, inc=1, device_id={axis: place}, device_id_type=MESH)

    @pl.when(has_low)
    def _():
        greet("ax", ax - 1)

    @pl.when(has_high)
    def _():
        greet("ax", ax + 1)

    @pl.when(has_inner)
    def _():
        greet("rad", rad - 1)

    @pl.when(has_outer)
    def _():
        greet("rad", rad + 1)

    for shift in range(1, sectors):
        greet("az", (az + shift) % sectors)

    def one(flag):
        return jnp.where(flag, 1, 0)

    pl.semaphore_wait(
        barrier,
        one(has_low) + one(has_high) + one(has_inner) + one(has_outer) + sectors - 1,
    )

    def remote(src, dst, send, recv, axis, place):
        return pltpu.make_async_remote_copy(
            src_ref=src,
            dst_ref=dst,
            send_sem=send,
            recv_sem=recv,
            device_id={axis: place},
            device_id_type=MESH,
        )

    def span(chunk):
        return pl.ds(bounds[chunk], bounds[chunk + 1] - bounds[chunk])

    def own(chunk):
        return pl.ds(PAD + bounds[chunk], bounds[chunk + 1] - bounds[chunk])

    def source(step, plane, chunk):
        if step == 0:
            return flow_ref.at[:, plane, span(chunk)]
        return state.at[step, :, plane, own(chunk)]

    def to_low(step, chunk):
        return remote(
            source(step, 0, chunk),
            high_plane.at[step, :, span(chunk)],
            low_send.at[step, chunk],
            low_recv.at[step, chunk],
            "ax",
            ax - 1,
        )

    def to_high(step, chunk):
        return remote(
            source(step, planes - 1, chunk),
            low_plane.at[step, :, span(chunk)],
            high_send.at[step, chunk],
            high_recv.at[step, chunk],
            "ax",
            ax + 1,
        )

    def to_right(step, chunk):
        return remote(
            edge_out.at[step, span(chunk)],
            edge_left.at[step, span(chunk)],
            right_send.at[step, chunk],
            right_recv.at[step, chunk],
            "az",
            right,
        )

    def to_left(step, chunk):
        return remote(
            edge_out.at[step, span(chunk)],
            edge_right.at[step, span(chunk)],
            left_send.at[step, chunk],
            left_recv.at[step, chunk],
            "az",
            left,
        )

    def to_inner(step):
        return remote(
            row_out.at[step, 0],
            row_in.at[step, 1],
            row_send.at[step, 0],
            row_recv.at[step, 0],
            "rad",
            rad - 1,
        )

    def to_outer(step):
        return remote(
            row_out.at[step, 1],
            row_in.at[step, 0],
            row_send.at[step, 1],
            row_recv.at[step, 1],
            "rad",
            rad + 1,
        )

    def to_opposite(step):
        return remote(
            row_out.at[step, 0],
            row_in.at[step, 0],
            opposite_send.at[step],
            opposite_recv.at[step],
            "az",
            partner,
        )

    def to_sector(step, shift):
        return remote(
            sum_out.at[step],
            sum_in.at[step, shift - 1],
            sum_send.at[step, shift - 1],
            sum_recv.at[step, shift - 1],
            "az",
            (az + shift) % sectors,
        )

    def send_planes(step, chunk):
        @pl.when(has_low)
        def _():
            to_low(step, chunk).start()

        @pl.when(has_high)
        def _():
            to_high(step, chunk).start()

    def send_edges(step, chunk):
        count = bounds[chunk + 1] - bounds[chunk]
        lane = lax.broadcasted_iota(jnp.int32, (count, columns), 1)
        packed = jnp.zeros((count, columns), jnp.float32)
        for block in range(blocks):
            values = state[step, block // planes, block % planes, own(chunk)]
            packed = jnp.where(
                lane // 2 == block, pltpu.roll(values, 2 * block + 1, 1), packed
            )
        edge_out[step, span(chunk)] = packed
        to_right(step, chunk).start()
        if sectors > 2:
            to_left(step, chunk).start()

    def send_first_row(step):
        for block in range(blocks):
            row_out[step, 0, pl.ds(block, 1)] = state[
                step, block // planes, block % planes, pl.ds(PAD, 1)
            ]

        @pl.when(has_inner)
        def _():
            to_inner(step).start()

        @pl.when(at_axis)
        def _():
            to_opposite(step).start()

    def send_last_row(step):
        for block in range(blocks):
            row_out[step, 1, pl.ds(block, 1)] = state[
                step, block // planes, block % planes, pl.ds(PAD + rows - 1, 1)
            ]

        @pl.when(has_outer)
        def _():
            to_outer(step).start()

    def receive_rows(step):
        @pl.when(has_inner)
        def _():
            to_outer(step).wait_recv()
            for block in range(blocks):
                state[step, block // planes, block % planes, pl.ds(PAD - 1, 1)] = row_in[
                    step, 0, pl.ds(block, 1)
                ]

        @pl.when(at_axis)
        def _():
            to_opposite(step).wait_recv()
            for block in range(blocks):
                sign = 1.0 if block // planes < 2 else -1.0
                state[step, block // planes, block % planes, pl.ds(PAD - 1, 1)] = (
                    sign * row_in[step, 0, pl.ds(block, 1)]
                )

        @pl.when(has_outer)
        def _():
            to_inner(step).wait_recv()
            for block in range(blocks):
                state[step, block // planes, block % planes, pl.ds(PAD + rows, 1)] = row_in[
                    step, 1, pl.ds(block, 1)
                ]

        @pl.when(jnp.logical_not(has_outer))
        def _():
            for block in range(blocks):
                state[step, block // planes, block % planes, pl.ds(PAD + rows, 1)] = jnp.zeros(
                    (1, columns), jnp.float32
                )

    def in_plane(step, chunk):
        to_right(step, chunk).wait_recv()
        if sectors > 2:
            to_left(step, chunk).wait_recv()
        for start in range(bounds[chunk], bounds[chunk + 1], 8):
            shape = (8, columns)
            lane = lax.broadcasted_iota(jnp.int32, shape, 1)
            row = lax.broadcasted_iota(jnp.int32, shape, 0)
            radius = (rad * rows + start + row).astype(jnp.float32) + 0.5
            reciprocal = 1.0 / radius
            arc = half_arc * reciprocal
            outer_weight = 1.0 + 0.5 * reciprocal
            inner_weight = 1.0 - 0.5 * reciprocal
            outer_flux = (0.5 * DT) * (1.0 + reciprocal)
            inner_flux = (0.5 * DT) * (1.0 - reciprocal)
            edges = edge_left[step, pl.ds(start, 8)]
            if sectors > 2:
                edges = jnp.where(lane % 2 == 0, edges, edge_right[step, pl.ds(start, 8)])

            def cell(channel, plane, offset=0):
                return state[step, channel, plane, pl.ds(PAD + start + offset, 8)]

            for plane in range(planes):
                center = [cell(c, plane) for c in range(channels)]
                outer = [cell(c, plane, 1) for c in range(channels)]
                inner = [cell(c, plane, -1) for c in range(channels)]
                ahead, behind = [], []
                for c in range(channels):
                    block = c * planes + plane
                    rim = pltpu.roll(edges, (columns - 2 * block - 1) % columns, 1)
                    ahead.append(
                        pltpu.roll(jnp.where(lane == 0, rim, center[c]), columns - 1, 1)
                    )
                    behind.append(
                        pltpu.roll(jnp.where(lane == columns - 1, rim, center[c]), 1, 1)
                    )
                level, axial, radial, swirl = center
                density = 1.0 + (RHO_RATIO - 1.0) * jnp.clip(level, 0.0, 1.0)
                thin = (DT * VISC) / density
                spread[plane, pl.ds(start, 8)] = thin
                laplace = [
                    outer_weight * outer[c] + inner_weight * inner[c] - 4.0 * center[c]
                    for c in range(channels)
                ]
                upper = lower = None
                if plane < planes - 1:
                    upper = [cell(c, plane + 1) for c in range(channels)]
                    laplace = [laplace[c] + upper[c] for c in range(channels)]
                if plane > 0:
                    lower = [cell(c, plane - 1) for c in range(channels)]
                    laplace = [laplace[c] + lower[c] for c in range(channels)]
                rate = (
                    (DT * KAPPA) * laplace[0]
                    - outer_flux * outer[2] * outer[0]
                    + inner_flux * inner[2] * inner[0]
                    - arc * (ahead[3] * ahead[0] - behind[3] * behind[0])
                )
                if upper is not None:
                    rate = rate - (0.5 * DT) * upper[1] * upper[0]
                if lower is not None:
                    rate = rate + (0.5 * DT) * lower[1] * lower[0]
                increment[0, plane, pl.ds(start, 8)] = rate
                drift = (0.5 * DT) * axial
                push = (0.5 * DT) * radial
                turn = arc * swirl
                for c in range(1, channels):
                    rate = (
                        thin * laplace[c]
                        - push * (outer[c] - inner[c])
                        - turn * (ahead[c] - behind[c])
                    )
                    if upper is not None:
                        rate = rate - drift * upper[c]
                    if lower is not None:
                        rate = rate + drift * lower[c]
                    if c == 2:
                        rate = rate + (DT * reciprocal) * swirl * swirl
                    if c == 3:
                        rate = rate - (DT * reciprocal) * swirl * radial
                    increment[c, plane, pl.ds(start, 8)] = rate

    def receive_planes(step, chunk):
        @pl.when(has_low)
        def _():
            to_high(step, chunk).wait_recv()

        @pl.when(has_high)
        def _():
            to_low(step, chunk).wait_recv()

    def add_planes(step, chunk):
        for plane, halo, sign in ((0, low_plane, 1.0), (planes - 1, high_plane, -1.0)):
            here = span(chunk)
            drift = (sign * 0.5 * DT) * state[step, 1, plane, own(chunk)]
            weight = drift + spread[plane, here]
            level = halo[step, 0, here]
            increment[0, plane, here] += level * (
                DT * KAPPA + (sign * 0.5 * DT) * halo[step, 1, here]
            )
            for c in range(1, channels):
                increment[c, plane, here] += weight * halo[step, c, here]

    def store(step, chunk):
        for c in range(channels):
            for plane in range(planes):
                value = state[step, c, plane, own(chunk)] + increment[c, plane, span(chunk)]
                if step == STEPS - 1:
                    out_ref[c, plane, span(chunk)] = value
                else:
                    state[step + 1, c, plane, own(chunk)] = value

    def widths(lane_shape):
        row = lax.broadcasted_iota(jnp.int32, lane_shape, 0)
        width = jnp.zeros(lane_shape, jnp.int32)
        for ring in range(rings):
            width = jnp.where(row == ring, width_ref[ring], width)
        return width

    def block_sums(step):
        shape = (rings, columns)
        lane = lax.broadcasted_iota(jnp.int32, shape, 1)
        width = widths(shape)
        values = [
            increment[block // planes, block % planes, pl.ds(0, rings)]
            for block in range(blocks)
        ]
        reach = 1
        while reach < columns:
            high_side = (lane // reach) % 2 == 1
            wide = width > reach
            values = [
                jnp.where(
                    wide,
                    value
                    + jnp.where(
                        high_side,
                        pltpu.roll(value, reach, 1),
                        pltpu.roll(value, columns - reach, 1),
                    ),
                    value,
                )
                for value in values
            ]
            reach *= 2
        packed = jnp.zeros(shape, jnp.float32)
        for block in range(blocks):
            increment[block // planes, block % planes, pl.ds(0, rings)] = values[block]
            packed = jnp.where(lane == block, values[block], packed)
        sum_out[step] = packed
        for shift in range(1, sectors):
            to_sector(step, shift).start()

    def block_means(step):
        shape = (rings, columns)
        width = widths(shape)
        far = jnp.zeros(shape, jnp.float32)
        for shift in range(1, sectors):
            to_sector(step, shift).wait_recv()
            sender = (az + sectors - shift) % sectors
            share = jnp.zeros(shape, jnp.float32)
            size = 2
            while size <= sectors:
                same = jnp.where(sender // size == az // size, 1.0, 0.0)
                share = jnp.where(width == size * columns, same, share)
                size *= 2
            far = far + share * sum_in[step, shift - 1]
        inverse = 1.0 / width.astype(jnp.float32)
        for block in range(blocks):
            here = (block // planes, block % planes, pl.ds(0, rings))
            total = increment[here] + jnp.broadcast_to(far[:, block : block + 1], shape)
            increment[here] = total * inverse

    for chunk in range(chunks):
        send_planes(0, chunk)
    for step in range(STEPS):

        @pl.when(jnp.logical_not(has_low))
        def _():
            low_plane[step] = jnp.zeros(low_plane.shape[1:], jnp.float32)

        @pl.when(jnp.logical_not(has_high))
        def _():
            high_plane[step] = jnp.zeros(high_plane.shape[1:], jnp.float32)

    load.wait()
    send_first_row(0)
    send_last_row(0)
    for chunk in range(chunks):
        send_edges(0, chunk)
    for step in range(STEPS):
        last = step == STEPS - 1
        receive_rows(step)
        for chunk in range(chunks):
            in_plane(step, chunk)
        order = range(chunks) if step == 0 else list(range(1, chunks)) + [0]

        def finish(chunk):
            store(step, chunk)
            if not last:
                send_planes(step + 1, chunk)
                send_edges(step + 1, chunk)
                if chunk == 0:
                    send_first_row(step + 1)
                if chunk == chunks - 1:
                    send_last_row(step + 1)

        for chunk in order:
            receive_planes(step, chunk)
            add_planes(step, chunk)
            if chunk == 0:

                @pl.when(at_axis)
                def _():
                    block_sums(step)

            else:
                finish(chunk)

        @pl.when(at_axis)
        def _():
            block_means(step)

        finish(0)

    for step in range(STEPS):
        for chunk in range(chunks):

            @pl.when(has_low)
            def _():
                to_low(step, chunk).wait_send()

            @pl.when(has_high)
            def _():
                to_high(step, chunk).wait_send()

            to_right(step, chunk).wait_send()
            if sectors > 2:
                to_left(step, chunk).wait_send()

        @pl.when(has_inner)
        def _():
            to_inner(step).wait_send()

        @pl.when(has_outer)
        def _():
            to_outer(step).wait_send()

        @pl.when(at_axis)
        def _():
            to_opposite(step).wait_send()
            for shift in range(1, sectors):
                to_sector(step, shift).wait_send()


def local(sizes, flow_state, cycle_widths):
    channels, planes, rows, columns = flow_state.shape
    rings = cycle_widths.shape[0]
    sectors = sizes[1]
    middle = rings + ((rows - rings) // 2 + 7) // 8 * 8
    bounds = (0, rings, middle, rows)
    chunks = len(bounds) - 1
    blocks = channels * planes
    f32 = jnp.float32
    dma = pltpu.SemaphoreType.DMA
    return pl.pallas_call(
        functools.partial(kernel, sizes, bounds),
        out_shape=jax.ShapeDtypeStruct(flow_state.shape, f32),
        in_specs=[
            pl.BlockSpec(memory_space=pl.ANY),
            pl.BlockSpec(memory_space=pltpu.SMEM),
        ],
        out_specs=pl.BlockSpec(memory_space=pltpu.VMEM),
        scratch_shapes=[
            pltpu.VMEM((STEPS, channels, planes, rows + 2 * PAD, columns), f32),
            pltpu.VMEM((channels, planes, rows, columns), f32),
            pltpu.VMEM((planes, rows, columns), f32),
            pltpu.VMEM((STEPS, channels, rows, columns), f32),
            pltpu.VMEM((STEPS, channels, rows, columns), f32),
            pltpu.VMEM((STEPS, rows, columns), f32),
            pltpu.VMEM((STEPS, rows, columns), f32),
            pltpu.VMEM((STEPS, rows, columns), f32),
            pltpu.VMEM((STEPS, 2, blocks, columns), f32),
            pltpu.VMEM((STEPS, 2, blocks, columns), f32),
            pltpu.VMEM((STEPS, rings, columns), f32),
            pltpu.VMEM((STEPS, sectors - 1, rings, columns), f32),
            dma,
            dma((STEPS, chunks)),
            dma((STEPS, chunks)),
            dma((STEPS, chunks)),
            dma((STEPS, chunks)),
            dma((STEPS, chunks)),
            dma((STEPS, chunks)),
            dma((STEPS, chunks)),
            dma((STEPS, chunks)),
            dma((STEPS, 2)),
            dma((STEPS, 2)),
            dma((STEPS,)),
            dma((STEPS,)),
            dma((STEPS, sectors - 1)),
            dma((STEPS, sectors - 1)),
        ],
        compiler_params=pltpu.CompilerParams(
            collective_id=0, has_side_effects=True, vmem_limit_bytes=32 * 1024 * 1024
        ),
    )(flow_state, cycle_widths)


def solution(mesh):
    sizes = (mesh.shape["ax"], mesh.shape["az"], mesh.shape["rad"])
    return jax.shard_map(
        functools.partial(local, sizes),
        mesh=mesh,
        in_specs=(P(None, ("groups", "ax"), "rad", "az"), P()),
        out_specs=P(None, ("groups", "ax"), "rad", "az"),
        check_vma=False,
    )
```

time: 373 us -> 20.1 us (0.05)
  local copies, waits for them, and re-layouts: 308 us -> 2.26 us
  starting transfers between devices: 25 us -> 0 us
  blocking collectives: 19.2 us -> 0 us
  Pallas kernels: 0 us -> 17.7 us
  waiting for transfers between devices: 13 us -> 0 us
  other arithmetic: 7.46 us -> 0 us
    gather x4 -> x0, local copies, waits for them, and re-layouts: 305 us -> none  [the longest x2 153 us: local(): jnp.take_along_axis(running, jnp.broadcast_to(block_start + local_width,...]
    ppermute x12 -> x0, starting transfers between devices: 25 us -> none  [the longest x6 16.8 us: extended_2(): lax.ppermute(lax.slice_in_dim(block, block.shape[dim] - width, None, axis...]
    all_gather x4 -> x0, blocking collectives: 19.2 us -> none  [the longest x2 10.5 us: local(): full_cycle = lax.all_gather(innermost, 'az', axis=2, tiled=True)]
    pallas_call x0 -> x1, Pallas kernels: none -> 17.7 us  [local(): pl.pallas_call(functools.partial(kernel, sizes, bounds), out_shape=jax.Sh...]
    ppermute x12 -> x0, waiting for transfers between devices: 13 us -> none  [the longest x6 7.62 us: extended_2(): lax.ppermute(lax.slice_in_dim(block, block.shape[dim] - width, None, axis...]
    another operation x2 -> x0, other arithmetic: 4.55 us -> none  [local(): running = jnp.concatenate([leading, jnp.cumsum(cycle_head, axis=3)], 3)]
  transfers between devices with their start and end apart: 12 -> 0, of which waited for: 3 -> 0; matrix products, arithmetic and copies ran while one was open for 1% -> 0% of each run, Pallas kernels for 0% -> 0%
where the time goes in v1:
time: 20.1 us; the launch traced here: 20 us
  Pallas kernels  17.7 us (88%)
  local copies, waits for them, and re-layouts  2.26 us (11%)
    pallas_call x1, Pallas kernels, local(): pl.pallas_call(functools.partial(kernel, sizes, bounds), out_shape=jax.Sh...  17.7 us
    unnamed x5, local copies, waits for them, and re-layouts  2.26 us

profile of v1, /device:TPU:0, one launch (start us, length us, event | category | flops | bytes accessed | tf_op | source)
XLA Modules:
  0.0 20.0 jit_solution(1545062014103634989)
XLA Ops:
  0.0 0.0 copy-start
  0.0 0.9 %copy-done = f32[4,2,48,128]{3,2,1,0:T(8,128)S(1)} copy-done((f32[4,2,48,128]{3,2,1,0:T(8,128)S(1)}, f32[4,2,48,128]{3,2,1,0:T(8,128)}, u32[]{:S(2)}) %copy-start) | copy-done | bytes 196632
  0.9 0.0 copy-start.1
  0.9 0.7 %copy-done.1 = s32[8]{0:T(128)S(1)} copy-done((s32[8]{0:T(128)S(1)}, s32[8]{0:T(128)}, u32[]{:S(2)}) %copy-start.1) | copy-done | bytes 56
  1.6 17.7 %shard_map.28 = f32[4,2,48,128]{3,2,1,0:T(8,128)S(1)} custom-call(f32[4,2,48,128]{3,2,1,0:T(8,128)S(1)} %copy-done, s32[8]{0:T(128)S(1)} %copy-done.1), custom_call_target="tpu_custom_call" | custom-call | tf_op jit(solution)/shard_map/pallas_call | solution.py:555
  19.3 0.7 %copy.4 = f32[4,2,48,128]{3,2,1,0:T(8,128)} copy(f32[4,2,48,128]{3,2,1,0:T(8,128)S(1)} %shard_map.28) | data formatting | bytes 393216
Async XLA Ops:
  0.0 0.9 %copy-start = (f32[4,2,48,128]{3,2,1,0:T(8,128)S(1)}, f32[4,2,48,128]{3,2,1,0:T(8,128)}, u32[]{:S(2)}) copy-start(f32[4,2,48,128]{3,2,1,0:T(8,128)} %flow_ref.1) | copy-start | bytes 589828
  0.9 0.7 %copy-start.1 = (s32[8]{0:T(128)S(1)}, s32[8]{0:T(128)}, u32[]{:S(2)}) copy-start(s32[8]{0:T(128)} %width_ref.1) | copy-start | bytes 100

commit v2 on v1

v2 whole, which is shorter than its diff:
```python
import functools
import math

import jax
import jax.numpy as jnp
from jax import lax
from jax.experimental import pallas as pl
from jax.experimental.pallas import tpu as pltpu
from jax.sharding import PartitionSpec as P

STEPS = 2
DT = 0.2
KAPPA = 0.05
VISC = 0.1
RHO_RATIO = 20.0
PAD = 8
MESH = pl.DeviceIdType.MESH


def kernel(
    sizes,
    bounds,
    flow_ref,
    width_ref,
    out_ref,
    result,
    state,
    increment,
    spread,
    low_plane,
    high_plane,
    edge_out,
    edge_left,
    edge_right,
    row_out,
    row_in,
    circle,
    circle_increment,
    circle_spread,
    circle_low,
    circle_high,
    rim_in,
    basis,
    width_smem,
    load_sem,
    width_sem,
    circle_sem,
    out_sem,
    low_send,
    low_recv,
    high_send,
    high_recv,
    left_send,
    left_recv,
    right_send,
    right_recv,
    row_send,
    row_recv,
    gather_send,
    gather_recv,
    corner_low_send,
    corner_low_recv,
    corner_high_send,
    corner_high_recv,
    rim_send,
    rim_recv,
):
    axials, sectors, rads = sizes
    channels, planes, rows, columns = flow_ref.shape
    blocks = channels * planes
    rings = width_ref.shape[0]
    around = sectors * columns
    chunks = len(bounds) - 1
    ax = lax.axis_index("ax")
    az = lax.axis_index("az")
    rad = lax.axis_index("rad")
    angle_step = 2.0 * math.pi / (sectors * columns)
    half_arc = DT / (2.0 * angle_step)
    has_low = ax > 0
    has_high = ax < axials - 1
    has_inner = rad > 0
    has_outer = rad < rads - 1
    at_axis = rad == 0
    left = (az + sectors - 1) % sectors
    right = (az + 1) % sectors

    load = pltpu.make_async_copy(
        flow_ref, state.at[0, :, :, pl.ds(PAD, rows)], load_sem
    )
    load.start()
    load_width = pltpu.make_async_copy(width_ref, width_smem, width_sem)
    load_width.start()
    load_circle = pltpu.make_async_copy(
        flow_ref.at[:, :, pl.ds(0, rings + 8)],
        circle.at[0, :, :, pl.ds(PAD, rings + 8), pl.ds(0, columns)],
        circle_sem,
    )
    load_circle.start()

    barrier = pltpu.get_barrier_semaphore()

    def greet(axis, place):
        pl.semaphore_signal(barrier, inc=1, device_id={axis: place}, device_id_type=MESH)

    def greet_corner(place, shift):
        pl.semaphore_signal(
            barrier,
            inc=1,
            device_id={"ax": place, "az": (az + shift) % sectors},
            device_id_type=MESH,
        )

    @pl.when(has_low)
    def _():
        greet("ax", ax - 1)

    @pl.when(has_high)
    def _():
        greet("ax", ax + 1)

    @pl.when(has_inner)
    def _():
        greet("rad", rad - 1)

    @pl.when(has_outer)
    def _():
        greet("rad", rad + 1)

    for shift in range(1, sectors):
        greet("az", (az + shift) % sectors)

    @pl.when(jnp.logical_and(at_axis, has_low))
    def _():
        for shift in range(1, sectors):
            greet_corner(ax - 1, shift)

    @pl.when(jnp.logical_and(at_axis, has_high))
    def _():
        for shift in range(1, sectors):
            greet_corner(ax + 1, shift)

    def one(flag):
        return jnp.where(flag, 1, 0)

    pl.semaphore_wait(
        barrier,
        one(has_low)
        + one(has_high)
        + one(has_inner)
        + one(has_outer)
        + sectors
        - 1
        + one(at_axis) * (one(has_low) + one(has_high)) * (sectors - 1),
    )

    def remote(src, dst, send, recv, axis, place):
        return pltpu.make_async_remote_copy(
            src_ref=src,
            dst_ref=dst,
            send_sem=send,
            recv_sem=recv,
            device_id={axis: place},
            device_id_type=MESH,
        )

    def span(chunk):
        return pl.ds(bounds[chunk], bounds[chunk + 1] - bounds[chunk])

    def own(chunk):
        return pl.ds(PAD + bounds[chunk], bounds[chunk + 1] - bounds[chunk])

    def source(step, plane, chunk):
        if step == 0:
            return flow_ref.at[:, plane, span(chunk)]
        return state.at[step, :, plane, own(chunk)]

    def to_low(step, chunk):
        return remote(
            source(step, 0, chunk),
            high_plane.at[step, :, span(chunk)],
            low_send.at[step, chunk],
            low_recv.at[step, chunk],
            "ax",
            ax - 1,
        )

    def to_high(step, chunk):
        return remote(
            source(step, planes - 1, chunk),
            low_plane.at[step, :, span(chunk)],
            high_send.at[step, chunk],
            high_recv.at[step, chunk],
            "ax",
            ax + 1,
        )

    def to_right(step, chunk):
        return remote(
            edge_out.at[step, span(chunk)],
            edge_left.at[step, span(chunk)],
            right_send.at[step, chunk],
            right_recv.at[step, chunk],
            "az",
            right,
        )

    def to_left(step, chunk):
        return remote(
            edge_out.at[step, span(chunk)],
            edge_right.at[step, span(chunk)],
            left_send.at[step, chunk],
            left_recv.at[step, chunk],
            "az",
            left,
        )

    def to_inner(step):
        return remote(
            row_out.at[step, 0],
            row_in.at[step, 1],
            row_send.at[step, 0],
            row_recv.at[step, 0],
            "rad",
            rad - 1,
        )

    def to_outer(step):
        return remote(
            row_out.at[step, 1],
            row_in.at[step, 0],
            row_send.at[step, 1],
            row_recv.at[step, 1],
            "rad",
            rad + 1,
        )

    def circle_source(step, plane):
        if step == 0:
            return flow_ref.at[:, plane, pl.ds(0, rings)]
        return circle.at[step, :, plane, pl.ds(PAD, rings)]

    def circle_target(ref, step):
        if step == 0:
            return ref.at[step, :, :, pl.ds(0, columns)]
        return ref.at[step]

    def circle_to_low(step):
        return remote(
            circle_source(step, 0),
            circle_target(circle_high, step),
            low_send.at[step, 0],
            low_recv.at[step, 0],
            "ax",
            ax - 1,
        )

    def circle_to_high(step):
        return remote(
            circle_source(step, planes - 1),
            circle_target(circle_low, step),
            high_send.at[step, 0],
            high_recv.at[step, 0],
            "ax",
            ax + 1,
        )

    def corner_to_low(shift):
        return pltpu.make_async_remote_copy(
            src_ref=flow_ref.at[:, 0, pl.ds(0, rings)],
            dst_ref=circle_high.at[0, :, :, pl.ds((sectors - shift) * columns, columns)],
            send_sem=corner_low_send.at[shift - 1],
            recv_sem=corner_low_recv.at[shift - 1],
            device_id={"ax": ax - 1, "az": (az + shift) % sectors},
            device_id_type=MESH,
        )

    def corner_to_high(shift):
        return pltpu.make_async_remote_copy(
            src_ref=flow_ref.at[:, planes - 1, pl.ds(0, rings)],
            dst_ref=circle_low.at[0, :, :, pl.ds((sectors - shift) * columns, columns)],
            send_sem=corner_high_send.at[shift - 1],
            recv_sem=corner_high_recv.at[shift - 1],
            device_id={"ax": ax + 1, "az": (az + shift) % sectors},
            device_id_type=MESH,
        )

    def gather(shift):
        return remote(
            flow_ref.at[:, :, pl.ds(0, rings + 8)],
            circle.at[
                0, :, :, pl.ds(PAD, rings + 8), pl.ds((sectors - shift) * columns, columns)
            ],
            gather_send.at[shift - 1],
            gather_recv.at[shift - 1],
            "az",
            (az + shift) % sectors,
        )

    def to_rim(step, shift):
        return remote(
            row_out.at[step, 0],
            rim_in.at[step, sectors - shift - 1],
            rim_send.at[step, shift - 1],
            rim_recv.at[step, shift - 1],
            "az",
            (az + shift) % sectors,
        )

    def send_circle(step):
        @pl.when(has_low)
        def _():
            circle_to_low(step).start()
            if step == 0:
                for shift in range(1, sectors):
                    corner_to_low(shift).start()

        @pl.when(has_high)
        def _():
            circle_to_high(step).start()
            if step == 0:
                for shift in range(1, sectors):
                    corner_to_high(shift).start()

    def receive_circle(step):
        @pl.when(has_low)
        def _():
            circle_to_high(step).wait_recv()
            if step == 0:
                for shift in range(1, sectors):
                    corner_to_high(shift).wait_recv()

        @pl.when(has_high)
        def _():
            circle_to_low(step).wait_recv()
            if step == 0:
                for shift in range(1, sectors):
                    corner_to_low(shift).wait_recv()

    def send_rim(step):
        for block in range(blocks):
            row = state[step, block // planes, block % planes, pl.ds(PAD + rings, 1)]
            row_out[step, 0, pl.ds(block, 1)] = row
            circle[
                step, block // planes, block % planes, pl.ds(PAD + rings, 1), pl.ds(0, columns)
            ] = row
        for shift in range(1, sectors):
            to_rim(step, shift).start()

    def receive_rim(step):
        for shift in range(1, sectors):
            to_rim(step, shift).wait_recv()
            place = sectors - shift
            for block in range(blocks):
                circle[
                    step,
                    block // planes,
                    block % planes,
                    pl.ds(PAD + rings, 1),
                    pl.ds(place * columns, columns),
                ] = rim_in[step, place - 1, pl.ds(block, 1)]

    def send_planes(step, chunk):
        @pl.when(has_low)
        def _():
            to_low(step, chunk).start()

        @pl.when(has_high)
        def _():
            to_high(step, chunk).start()

    def send_edges(step, chunk):
        count = bounds[chunk + 1] - bounds[chunk]
        lane = lax.broadcasted_iota(jnp.int32, (count, columns), 1)
        packed = jnp.zeros((count, columns), jnp.float32)
        for block in range(blocks):
            values = state[step, block // planes, block % planes, own(chunk)]
            packed = jnp.where(
                lane // 2 == block, pltpu.roll(values, 2 * block + 1, 1), packed
            )
        edge_out[step, span(chunk)] = packed
        to_right(step, chunk).start()
        if sectors > 2:
            to_left(step, chunk).start()

    def send_first_row(step):
        for block in range(blocks):
            row_out[step, 0, pl.ds(block, 1)] = state[
                step, block // planes, block % planes, pl.ds(PAD, 1)
            ]

        to_inner(step).start()

    def send_last_row(step):
        for block in range(blocks):
            row_out[step, 1, pl.ds(block, 1)] = state[
                step, block // planes, block % planes, pl.ds(PAD + rows - 1, 1)
            ]

        @pl.when(has_outer)
        def _():
            to_outer(step).start()

    def receive_rows(step):
        @pl.when(has_inner)
        def _():
            to_outer(step).wait_recv()
            for block in range(blocks):
                state[step, block // planes, block % planes, pl.ds(PAD - 1, 1)] = row_in[
                    step, 0, pl.ds(block, 1)
                ]

        @pl.when(has_outer)
        def _():
            to_inner(step).wait_recv()
            for block in range(blocks):
                state[step, block // planes, block % planes, pl.ds(PAD + rows, 1)] = row_in[
                    step, 1, pl.ds(block, 1)
                ]

        @pl.when(jnp.logical_not(has_outer))
        def _():
            for block in range(blocks):
                state[step, block // planes, block % planes, pl.ds(PAD + rows, 1)] = jnp.zeros(
                    (1, columns), jnp.float32
                )

    def terms(start, shape):
        row = lax.broadcasted_iota(jnp.int32, shape, 0)
        radius = (rad * rows + start + row).astype(jnp.float32) + 0.5
        reciprocal = 1.0 / radius
        return (
            reciprocal,
            half_arc * reciprocal,
            1.0 + 0.5 * reciprocal,
            1.0 - 0.5 * reciprocal,
            (0.5 * DT) * (1.0 + reciprocal),
            (0.5 * DT) * (1.0 - reciprocal),
        )

    def plane_rates(weights, center, outer, inner, ahead, behind, upper, lower):
        reciprocal, arc, outer_weight, inner_weight, outer_flux, inner_flux = weights
        level, axial, radial, swirl = center
        density = 1.0 + (RHO_RATIO - 1.0) * jnp.clip(level, 0.0, 1.0)
        thin = (DT * VISC) / density
        laplace = [
            outer_weight * outer[c] + inner_weight * inner[c] - 4.0 * center[c]
            for c in range(channels)
        ]
        for other in (upper, lower):
            if other is not None:
                laplace = [laplace[c] + other[c] for c in range(channels)]
        rate = (
            (DT * KAPPA) * laplace[0]
            - outer_flux * outer[2] * outer[0]
            + inner_flux * inner[2] * inner[0]
            - arc * (ahead[3] * ahead[0] - behind[3] * behind[0])
        )
        if upper is not None:
            rate = rate - (0.5 * DT) * upper[1] * upper[0]
        if lower is not None:
            rate = rate + (0.5 * DT) * lower[1] * lower[0]
        found = [rate]
        drift = (0.5 * DT) * axial
        push = (0.5 * DT) * radial
        turn = arc * swirl
        for c in range(1, channels):
            rate = (
                thin * laplace[c]
                - push * (outer[c] - inner[c])
                - turn * (ahead[c] - behind[c])
            )
            if upper is not None:
                rate = rate - drift * upper[c]
            if lower is not None:
                rate = rate + drift * lower[c]
            if c == 2:
                rate = rate + (DT * reciprocal) * swirl * swirl
            if c == 3:
                rate = rate - (DT * reciprocal) * swirl * radial
            found.append(rate)
        return thin, found

    def in_plane(step, chunk):
        to_right(step, chunk).wait_recv()
        if sectors > 2:
            to_left(step, chunk).wait_recv()
        for start in range(bounds[chunk], bounds[chunk + 1], 8):
            shape = (8, columns)
            lane = lax.broadcasted_iota(jnp.int32, shape, 1)
            weights = terms(start, shape)
            edges = edge_left[step, pl.ds(start, 8)]
            if sectors > 2:
                edges = jnp.where(lane % 2 == 0, edges, edge_right[step, pl.ds(start, 8)])

            def cell(channel, plane, offset=0):
                return state[step, channel, plane, pl.ds(PAD + start + offset, 8)]

            def cells(plane, offset=0):
                return [cell(c, plane, offset) for c in range(channels)]

            for plane in range(planes):
                center = cells(plane)
                ahead, behind = [], []
                for c in range(channels):
                    block = c * planes + plane
                    rim = pltpu.roll(edges, (columns - 2 * block - 1) % columns, 1)
                    ahead.append(
                        pltpu.roll(jnp.where(lane == 0, rim, center[c]), columns - 1, 1)
                    )
                    behind.append(
                        pltpu.roll(jnp.where(lane == columns - 1, rim, center[c]), 1, 1)
                    )
                thin, rate = plane_rates(
                    weights,
                    center,
                    cells(plane, 1),
                    cells(plane, -1),
                    ahead,
                    behind,
                    cells(plane + 1) if plane < planes - 1 else None,
                    cells(plane - 1) if plane > 0 else None,
                )
                spread[plane, pl.ds(start, 8)] = thin
                for c in range(channels):
                    increment[c, plane, pl.ds(start, 8)] = rate[c]

    def in_circle(step):
        if step == 0:
            load_circle.wait()
            for shift in range(1, sectors):
                gather(shift).wait_recv()
        else:
            receive_rim(step)
        for c in range(channels):
            sign = 1.0 if c < 2 else -1.0
            for plane in range(planes):
                first = circle[step, c, plane, pl.ds(PAD, 8)]
                circle[step, c, plane, pl.ds(PAD - 1, 1)] = (
                    sign * pltpu.roll(first, around // 2, 1)[:1]
                )
        for start in range(0, rings, 8):
            weights = terms(start, (8, around))

            def cells(plane, offset=0):
                return [
                    circle[step, c, plane, pl.ds(PAD + start + offset, 8)]
                    for c in range(channels)
                ]

            for plane in range(planes):
                center = cells(plane)
                thin, rate = plane_rates(
                    weights,
                    center,
                    cells(plane, 1),
                    cells(plane, -1),
                    [pltpu.roll(x, around - 1, 1) for x in center],
                    [pltpu.roll(x, 1, 1) for x in center],
                    cells(plane + 1) if plane < planes - 1 else None,
                    cells(plane - 1) if plane > 0 else None,
                )
                circle_spread[plane, pl.ds(start, 8)] = thin
                for c in range(channels):
                    circle_increment[c, plane, pl.ds(start, 8)] = rate[c]

    def receive_planes(step, chunk):
        @pl.when(has_low)
        def _():
            to_high(step, chunk).wait_recv()

        @pl.when(has_high)
        def _():
            to_low(step, chunk).wait_recv()

    def add_planes(step, chunk):
        for plane, halo, sign in ((0, low_plane, 1.0), (planes - 1, high_plane, -1.0)):
            here = span(chunk)
            drift = (sign * 0.5 * DT) * state[step, 1, plane, own(chunk)]
            weight = drift + spread[plane, here]
            level = halo[step, 0, here]
            increment[0, plane, here] += level * (
                DT * KAPPA + (sign * 0.5 * DT) * halo[step, 1, here]
            )
            for c in range(1, channels):
                increment[c, plane, here] += weight * halo[step, c, here]

    def store(step, chunk):
        for c in range(channels):
            for plane in range(planes):
                value = state[step, c, plane, own(chunk)] + increment[c, plane, span(chunk)]
                if step == STEPS - 1:
                    result[c, plane, span(chunk)] = value
                else:
                    state[step + 1, c, plane, own(chunk)] = value

    def add_circle(step):
        for plane, halo, sign in ((0, circle_low, 1.0), (planes - 1, circle_high, -1.0)):
            drift = (sign * 0.5 * DT) * circle[step, 1, plane, pl.ds(PAD, rings)]
            weight = drift + circle_spread[plane]
            circle_increment[0, plane] += halo[step, 0] * (
                DT * KAPPA + (sign * 0.5 * DT) * halo[step, 1]
            )
            for c in range(1, channels):
                circle_increment[c, plane] += weight * halo[step, c]

    level_count = columns.bit_length() - 1

    def make_basis():
        for level in range(level_count):
            width = 2 << level
            shape = (2 * columns, columns)
            row = lax.broadcasted_iota(jnp.int32, shape, 0) % columns
            lane = lax.broadcasted_iota(jnp.int32, shape, 1)
            same = jnp.where(row // width == lane // width, 1.0 / width, 0.0)
            basis[:, pl.ds(level * columns, columns)] = same.astype(jnp.bfloat16)

    def block_means(step):
        shape = (8, columns)
        row = lax.broadcasted_iota(jnp.int32, shape, 0)
        for start in range(0, rings, 8):
            width = jnp.zeros(shape, jnp.int32)
            for ring in range(8):
                width = jnp.where(row == ring, width_smem[start + ring], width)
            values = jnp.concatenate(
                [
                    circle_increment[
                        block // planes,
                        block % planes,
                        pl.ds(start, 8),
                        pl.ds(sector * columns, columns),
                    ]
                    for block in range(blocks)
                    for sector in range(sectors)
                ],
                axis=0,
            )
            coarse = values.astype(jnp.bfloat16)
            fine = (values - coarse.astype(jnp.float32)).astype(jnp.bfloat16)
            means = jnp.dot(
                jnp.concatenate([coarse, fine], axis=1),
                basis[...],
                preferred_element_type=jnp.float32,
            )
            for block in range(blocks):
                picked, whole = [], []
                for sector in range(sectors):
                    first = (block * sectors + sector) * 8
                    mean = None
                    for level in range(level_count):
                        part = means[
                            first : first + 8, level * columns : (level + 1) * columns
                        ]
                        if mean is None:
                            mean = part
                        else:
                            mean = jnp.where(width == 2 << level, part, mean)
                    whole.append(part)
                    picked.append(mean)
                size = 2
                while size <= sectors:
                    for sector in range(sectors):
                        total = jnp.zeros(shape, jnp.float32)
                        for other in range(sectors):
                            if size == sectors:
                                total = total + whole[other]
                            else:
                                same = (az + sector) % sectors // size == (
                                    az + other
                                ) % sectors // size
                                total = total + jnp.where(same, 1.0, 0.0) * whole[other]
                        picked[sector] = jnp.where(
                            width == size * columns, total * (1.0 / size), picked[sector]
                        )
                    size *= 2
                c, plane = block // planes, block % planes
                here = pl.ds(PAD + start, 8)
                for sector in range(sectors):
                    lanes = pl.ds(sector * columns, columns)
                    if step == STEPS - 1 and sector > 0:
                        continue
                    value = circle[step, c, plane, here, lanes] + picked[sector]
                    if step == STEPS - 1:
                        result[c, plane, pl.ds(start, 8)] = value
                    else:
                        circle[step + 1, c, plane, here, lanes] = value
                        if sector == 0:
                            state[step + 1, c, plane, here] = value

    def unload(chunk):
        return pltpu.make_async_copy(
            result.at[:, :, span(chunk)], out_ref.at[:, :, span(chunk)], out_sem.at[chunk]
        )

    off_axis = jnp.logical_not(at_axis)

    @pl.when(at_axis)
    def _():
        send_circle(0)
        for shift in range(1, sectors):
            gather(shift).start()

    @pl.when(off_axis)
    def _():
        send_planes(0, 0)

    for chunk in range(1, chunks):
        send_planes(0, chunk)

    @pl.when(jnp.logical_not(has_low))
    def _():
        low_plane[...] = jnp.zeros(low_plane.shape, jnp.float32)
        circle_low[...] = jnp.zeros(circle_low.shape, jnp.float32)

    @pl.when(jnp.logical_not(has_high))
    def _():
        high_plane[...] = jnp.zeros(high_plane.shape, jnp.float32)
        circle_high[...] = jnp.zeros(circle_high.shape, jnp.float32)

    load.wait()
    send_last_row(0)

    @pl.when(off_axis)
    def _():
        send_first_row(0)
        send_edges(0, 0)

    for chunk in range(1, chunks):
        send_edges(0, chunk)

    @pl.when(at_axis)
    def _():
        make_basis()

    load_width.wait()
    for step in range(STEPS):
        last = step == STEPS - 1
        receive_rows(step)

        @pl.when(at_axis)
        def _():
            in_circle(step)
            receive_circle(step)
            add_circle(step)
            block_means(step)
            if last:
                unload(0).start()
            else:
                send_circle(step + 1)

        @pl.when(off_axis)
        def _():
            in_plane(step, 0)

        for chunk in range(1, chunks):
            in_plane(step, chunk)

        @pl.when(off_axis)
        def _():
            receive_planes(step, 0)
            add_planes(step, 0)
            store(step, 0)
            if last:
                unload(0).start()
            else:
                send_planes(step + 1, 0)
                send_edges(step + 1, 0)
                send_first_row(step + 1)

        for chunk in range(1, chunks):
            receive_planes(step, chunk)
            add_planes(step, chunk)
            store(step, chunk)
            if last:
                unload(chunk).start()
            else:
                send_planes(step + 1, chunk)
                send_edges(step + 1, chunk)
                if chunk == 1:

                    @pl.when(at_axis)
                    def _():
                        send_rim(step + 1)

                if chunk == chunks - 1:
                    send_last_row(step + 1)

    @pl.when(off_axis)
    def _():
        load_circle.wait()

    for step in range(STEPS):
        for chunk in range(chunks):

            def sent():
                @pl.when(has_low)
                def _():
                    to_low(step, chunk).wait_send()

                @pl.when(has_high)
                def _():
                    to_high(step, chunk).wait_send()

                to_right(step, chunk).wait_send()
                if sectors > 2:
                    to_left(step, chunk).wait_send()

            if chunk == 0:
                pl.when(off_axis)(sent)
            else:
                sent()

        @pl.when(has_inner)
        def _():
            to_inner(step).wait_send()

        @pl.when(has_outer)
        def _():
            to_outer(step).wait_send()

        @pl.when(at_axis)
        def _():
            @pl.when(has_low)
            def _():
                circle_to_low(step).wait_send()
                if step == 0:
                    for shift in range(1, sectors):
                        corner_to_low(shift).wait_send()

            @pl.when(has_high)
            def _():
                circle_to_high(step).wait_send()
                if step == 0:
                    for shift in range(1, sectors):
                        corner_to_high(shift).wait_send()

            for shift in range(1, sectors):
                if step == 0:
                    gather(shift).wait_send()
                else:
                    to_rim(step, shift).wait_send()

    for chunk in range(chunks):
        unload(chunk).wait()


def local(sizes, flow_state, cycle_widths):
    channels, planes, rows, columns = flow_state.shape
    rings = cycle_widths.shape[0]
    sectors = sizes[1]
    middle = rings + ((rows - rings) // 2 + 7) // 8 * 8
    bounds = (0, rings, middle, rows)
    chunks = len(bounds) - 1
    blocks = channels * planes
    around = sectors * columns
    f32 = jnp.float32
    dma = pltpu.SemaphoreType.DMA
    return pl.pallas_call(
        functools.partial(kernel, sizes, bounds),
        out_shape=jax.ShapeDtypeStruct(flow_state.shape, f32),
        in_specs=[
            pl.BlockSpec(memory_space=pl.ANY),
            pl.BlockSpec(memory_space=pl.ANY),
        ],
        out_specs=pl.BlockSpec(memory_space=pl.ANY),
        scratch_shapes=[
            pltpu.VMEM((channels, planes, rows, columns), f32),
            pltpu.VMEM((STEPS, channels, planes, rows + 2 * PAD, columns), f32),
            pltpu.VMEM((channels, planes, rows, columns), f32),
            pltpu.VMEM((planes, rows, columns), f32),
            pltpu.VMEM((STEPS, channels, rows, columns), f32),
            pltpu.VMEM((STEPS, channels, rows, columns), f32),
            pltpu.VMEM((STEPS, rows, columns), f32),
            pltpu.VMEM((STEPS, rows, columns), f32),
            pltpu.VMEM((STEPS, rows, columns), f32),
            pltpu.VMEM((STEPS, 2, blocks, columns), f32),
            pltpu.VMEM((STEPS, 2, blocks, columns), f32),
            pltpu.VMEM((STEPS, channels, planes, rings + 2 * PAD, around), f32),
            pltpu.VMEM((channels, planes, rings, around), f32),
            pltpu.VMEM((planes, rings, around), f32),
            pltpu.VMEM((STEPS, channels, rings, around), f32),
            pltpu.VMEM((STEPS, channels, rings, around), f32),
            pltpu.VMEM((STEPS, sectors - 1, blocks, columns), f32),
            pltpu.VMEM((2 * columns, (columns.bit_length() - 1) * columns), jnp.bfloat16),
            pltpu.SMEM((rings,), jnp.int32),
            dma,
            dma,
            dma,
            dma((chunks,)),
            dma((STEPS, chunks)),
            dma((STEPS, chunks)),
            dma((STEPS, chunks)),
            dma((STEPS, chunks)),
            dma((STEPS, chunks)),
            dma((STEPS, chunks)),
            dma((STEPS, chunks)),
            dma((STEPS, chunks)),
            dma((STEPS, 2)),
            dma((STEPS, 2)),
            dma((sectors - 1,)),
            dma((sectors - 1,)),
            dma((sectors - 1,)),
            dma((sectors - 1,)),
            dma((sectors - 1,)),
            dma((sectors - 1,)),
            dma((STEPS, sectors - 1)),
            dma((STEPS, sectors - 1)),
        ],
        compiler_params=pltpu.CompilerParams(
            collective_id=0, has_side_effects=True, vmem_limit_bytes=64 * 1024 * 1024
        ),
    )(flow_state, cycle_widths)


def solution(mesh):
    sizes = (mesh.shape["ax"], mesh.shape["az"], mesh.shape["rad"])
    return jax.shard_map(
        functools.partial(local, sizes),
        mesh=mesh,
        in_specs=(P(None, ("groups", "ax"), "rad", "az"), P()),
        out_specs=P(None, ("groups", "ax"), "rad", "az"),
        check_vma=False,
    )
```

time: 20.1 us -> 15.4 us (0.77)
  Pallas kernels: 17.7 us -> 13.7 us
  local copies, waits for them, and re-layouts: 2.26 us -> 1.62 us
    pallas_call x1, Pallas kernels: 17.7 us -> 13.7 us  [local(): pl.pallas_call(functools.partial(kernel, sizes, bounds), out_shape=jax.Sh...]
    unnamed x5 -> x1, local copies, waits for them, and re-layouts: 2.26 us -> 1.62 us
where the time goes in v2:
time: 15.4 us; the launch traced here: 15.3 us
  Pallas kernels  13.7 us (89%)
  local copies, waits for them, and re-layouts  1.62 us (11%)
    pallas_call x1, Pallas kernels, local(): pl.pallas_call(functools.partial(kernel, sizes, bounds), out_shape=jax.Sh...  13.7 us
    unnamed x1, local copies, waits for them, and re-layouts  1.62 us

profile of v2, /device:TPU:0, one launch (start us, length us, event | category | flops | bytes accessed | tf_op | source)
XLA Modules:
  0.0 15.3 jit_solution(2442169377984165917)
XLA Ops:
  0.0 13.7 %shard_map.28 = f32[4,2,48,128]{3,2,1,0:T(8,128)} custom-call(f32[4,2,48,128]{3,2,1,0:T(8,128)} %flow_ref.1, s32[8]{0:T(128)} %width_ref.1), custom_call_target="tpu_custom_call" | custom-call | tf_op jit(solution)/shard_map/pallas_call | solution.py:857
  13.7 1.6 %copy.4 = f32[4,2,48,128]{3,2,1,0:T(8,128)} copy(f32[4,2,48,128]{3,2,1,0:T(8,128)} %shard_map.28) | data formatting | bytes 393216

commit v3 on v2

--- a/solution.py
+++ b/solution.py
@@ -23,7 +23,6 @@
     flow_ref,
     width_ref,
     out_ref,
-    result,
     state,
     increment,
     spread,
@@ -45,7 +44,6 @@
     load_sem,
     width_sem,
     circle_sem,
-    out_sem,
     low_send,
     low_recv,
     high_send,
@@ -589,7 +587,7 @@
             for plane in range(planes):
                 value = state[step, c, plane, own(chunk)] + increment[c, plane, span(chunk)]
                 if step == STEPS - 1:
-                    result[c, plane, span(chunk)] = value
+                    out_ref[c, plane, span(chunk)] = value
                 else:
                     state[step + 1, c, plane, own(chunk)] = value
 
@@ -680,17 +678,12 @@
                         continue
                     value = circle[step, c, plane, here, lanes] + picked[sector]
                     if step == STEPS - 1:
-                        result[c, plane, pl.ds(start, 8)] = value
+                        out_ref[c, plane, pl.ds(start, 8)] = value
                     else:
                         circle[step + 1, c, plane, here, lanes] = value
                         if sector == 0:
                             state[step + 1, c, plane, here] = value
 
-    def unload(chunk):
-        return pltpu.make_async_copy(
-            result.at[:, :, span(chunk)], out_ref.at[:, :, span(chunk)], out_sem.at[chunk]
-        )
-
     off_axis = jnp.logical_not(at_axis)
 
     @pl.when(at_axis)
@@ -742,9 +735,7 @@
             receive_circle(step)
             add_circle(step)
             block_means(step)
-            if last:
-                unload(0).start()
-            else:
+            if not last:
                 send_circle(step + 1)
 
         @pl.when(off_axis)
@@ -759,9 +750,7 @@
             receive_planes(step, 0)
             add_planes(step, 0)
             store(step, 0)
-            if last:
-                unload(0).start()
-            else:
+            if not last:
                 send_planes(step + 1, 0)
                 send_edges(step + 1, 0)
                 send_first_row(step + 1)
@@ -770,9 +759,7 @@
             receive_planes(step, chunk)
             add_planes(step, chunk)
             store(step, chunk)
-            if last:
-                unload(chunk).start()
-            else:
+            if not last:
                 send_planes(step + 1, chunk)
                 send_edges(step + 1, chunk)
                 if chunk == 1:
@@ -838,9 +825,6 @@
                     gather(shift).wait_send()
                 else:
                     to_rim(step, shift).wait_send()
-
-    for chunk in range(chunks):
-        unload(chunk).wait()
 
 
 def local(sizes, flow_state, cycle_widths):
@@ -856,14 +840,13 @@
     dma = pltpu.SemaphoreType.DMA
     return pl.pallas_call(
         functools.partial(kernel, sizes, bounds),
-        out_shape=jax.ShapeDtypeStruct(flow_state.shape, f32),
+        out_shape=pltpu.VMEM(flow_state.shape, f32),
         in_specs=[
             pl.BlockSpec(memory_space=pl.ANY),
             pl.BlockSpec(memory_space=pl.ANY),
         ],
-        out_specs=pl.BlockSpec(memory_space=pl.ANY),
+        out_specs=pl.BlockSpec(memory_space=pltpu.VMEM),
         scratch_shapes=[
-            pltpu.VMEM((channels, planes, rows, columns), f32),
             pltpu.VMEM((STEPS, channels, planes, rows + 2 * PAD, columns), f32),
             pltpu.VMEM((channels, planes, rows, columns), f32),
             pltpu.VMEM((planes, rows, columns), f32),
@@ -885,7 +868,6 @@
             dma,
             dma,
             dma,
-            dma((chunks,)),
             dma((STEPS, chunks)),
             dma((STEPS, chunks)),
             dma((STEPS, chunks)),
@@ -906,7 +888,7 @@
             dma((STEPS, sectors - 1)),
         ],
         compiler_params=pltpu.CompilerParams(
-            collective_id=0, has_side_effects=True, vmem_limit_bytes=64 * 1024 * 1024
+            collective_id=0, has_side_effects=True, vmem_limit_bytes=64 * 1024 * 1024 - 262144
         ),
     )(flow_state, cycle_widths)
 

time: 15.4 us -> 13.9 us (0.903)
  local copies, waits for them, and re-layouts: 1.62 us -> 0.68 us
  Pallas kernels: 13.7 us -> 13.1 us
    unnamed x1, local copies, waits for them, and re-layouts: 1.62 us -> 0.68 us
    pallas_call x1, Pallas kernels: 13.7 us -> 13.1 us  [local(): pl.pallas_call(functools.partial(kernel, sizes, bounds), out_shape=pltpu....]
where the time goes in v3:
time: 13.9 us; the launch traced here: 13.8 us
  Pallas kernels  13.1 us (94%)
  local copies, waits for them, and re-layouts  0.68 us (5%)
    pallas_call x1, Pallas kernels, local(): pl.pallas_call(functools.partial(kernel, sizes, bounds), out_shape=pltpu....  13.1 us
    unnamed x1, local copies, waits for them, and re-layouts  0.68 us

profile of v3, /device:TPU:0, one launch (start us, length us, event | category | flops | bytes accessed | tf_op | source)
XLA Modules:
  0.0 13.8 jit_solution(646766701961381175)
XLA Ops:
  0.0 13.1 %shard_map.28 = f32[4,2,48,128]{3,2,1,0:T(8,128)S(1)} custom-call(f32[4,2,48,128]{3,2,1,0:T(8,128)} %flow_ref.1, s32[8]{0:T(128)} %width_ref.1), custom_call_target="tpu_custom_call" | custom-call | tf_op jit(solution)/shard_map/pallas_call | solution.py:841
  13.1 0.7 %copy.4 = f32[4,2,48,128]{3,2,1,0:T(8,128)} copy(f32[4,2,48,128]{3,2,1,0:T(8,128)S(1)} %shard_map.28) | data formatting | bytes 393216

commit v4 on v3

--- a/solution.py
+++ b/solution.py
@@ -732,18 +732,21 @@
         @pl.when(at_axis)
         def _():
             in_circle(step)
+
+        @pl.when(off_axis)
+        def _():
+            in_plane(step, 0)
+
+        for chunk in range(1, chunks):
+            in_plane(step, chunk)
+
+        @pl.when(at_axis)
+        def _():
             receive_circle(step)
             add_circle(step)
             block_means(step)
             if not last:
                 send_circle(step + 1)
-
-        @pl.when(off_axis)
-        def _():
-            in_plane(step, 0)
-
-        for chunk in range(1, chunks):
-            in_plane(step, chunk)
 
         @pl.when(off_axis)
         def _():

time: 13.9 us -> 13.9 us (level)
  no operation moved by 1% of the time
where the time goes in v4:
time: 13.9 us; the launch traced here: 13.8 us
  Pallas kernels  13.1 us (94%)
  local copies, waits for them, and re-layouts  0.68 us (5%)
    pallas_call x1, Pallas kernels, local(): pl.pallas_call(functools.partial(kernel, sizes, bounds), out_shape=pltpu....  13.1 us
    unnamed x1, local copies, waits for them, and re-layouts  0.68 us

profile of v4, /device:TPU:0, one launch (start us, length us, event | category | flops | bytes accessed | tf_op | source)
XLA Modules:
  0.0 13.8 jit_solution(13653666765838654127)
XLA Ops:
  0.0 13.1 %shard_map.28 = f32[4,2,48,128]{3,2,1,0:T(8,128)S(1)} custom-call(f32[4,2,48,128]{3,2,1,0:T(8,128)} %flow_ref.1, s32[8]{0:T(128)} %width_ref.1), custom_call_target="tpu_custom_call" | custom-call | tf_op jit(solution)/shard_map/pallas_call | solution.py:844
  13.1 0.7 %copy.4 = f32[4,2,48,128]{3,2,1,0:T(8,128)} copy(f32[4,2,48,128]{3,2,1,0:T(8,128)S(1)} %shard_map.28) | data formatting | bytes 393216

commit v5 on v3

--- a/solution.py
+++ b/solution.py
@@ -732,11 +732,6 @@
         @pl.when(at_axis)
         def _():
             in_circle(step)
-            receive_circle(step)
-            add_circle(step)
-            block_means(step)
-            if not last:
-                send_circle(step + 1)
 
         @pl.when(off_axis)
         def _():
@@ -770,6 +765,14 @@
 
                 if chunk == chunks - 1:
                     send_last_row(step + 1)
+
+        @pl.when(at_axis)
+        def _():
+            receive_circle(step)
+            add_circle(step)
+            block_means(step)
+            if not last:
+                send_circle(step + 1)
 
     @pl.when(off_axis)
     def _():

time: 13.9 us -> 14.5 us (1.043)
  Pallas kernels: 13.1 us -> 13.6 us
    pallas_call x1, Pallas kernels: 13.1 us -> 13.6 us  [local(): pl.pallas_call(functools.partial(kernel, sizes, bounds), out_shape=pltpu....]
where the time goes in v5:
time: 14.5 us; the launch traced here: 14.3 us
  Pallas kernels  13.6 us (94%)
  local copies, waits for them, and re-layouts  0.68 us (5%)
    pallas_call x1, Pallas kernels, local(): pl.pallas_call(functools.partial(kernel, sizes, bounds), out_shape=pltpu....  13.6 us
    unnamed x1, local copies, waits for them, and re-layouts  0.68 us

profile of v5, /device:TPU:0, one launch (start us, length us, event | category | flops | bytes accessed | tf_op | source)
XLA Modules:
  0.0 14.3 jit_solution(10598430776315384725)
XLA Ops:
  0.0 13.6 %shard_map.28 = f32[4,2,48,128]{3,2,1,0:T(8,128)S(1)} custom-call(f32[4,2,48,128]{3,2,1,0:T(8,128)} %flow_ref.1, s32[8]{0:T(128)} %width_ref.1), custom_call_target="tpu_custom_call" | custom-call | tf_op jit(solution)/shard_map/pallas_call | solution.py:844
  13.6 0.7 %copy.4 = f32[4,2,48,128]{3,2,1,0:T(8,128)} copy(f32[4,2,48,128]{3,2,1,0:T(8,128)S(1)} %shard_map.28) | data formatting | bytes 393216

commit v6 on v3

--- a/solution.py
+++ b/solution.py
@@ -727,7 +727,6 @@
     load_width.wait()
     for step in range(STEPS):
         last = step == STEPS - 1
-        receive_rows(step)
 
         @pl.when(at_axis)
         def _():
@@ -737,6 +736,8 @@
             block_means(step)
             if not last:
                 send_circle(step + 1)
+
+        receive_rows(step)
 
         @pl.when(off_axis)
         def _():

time: 13.9 us -> 13.9 us (level)
  no operation moved by 1% of the time
where the time goes in v6:
time: 13.9 us; the launch traced here: 13.8 us
  Pallas kernels  13.1 us (94%)
  local copies, waits for them, and re-layouts  0.68 us (5%)
    pallas_call x1, Pallas kernels, local(): pl.pallas_call(functools.partial(kernel, sizes, bounds), out_shape=pltpu....  13.1 us
    unnamed x1, local copies, waits for them, and re-layouts  0.68 us

profile of v6, /device:TPU:0, one launch (start us, length us, event | category | flops | bytes accessed | tf_op | source)
XLA Modules:
  0.0 13.8 jit_solution(18396054419057380049)
XLA Ops:
  0.0 13.1 %shard_map.28 = f32[4,2,48,128]{3,2,1,0:T(8,128)S(1)} custom-call(f32[4,2,48,128]{3,2,1,0:T(8,128)} %flow_ref.1, s32[8]{0:T(128)} %width_ref.1), custom_call_target="tpu_custom_call" | custom-call | tf_op jit(solution)/shard_map/pallas_call | solution.py:842
  13.1 0.7 %copy.4 = f32[4,2,48,128]{3,2,1,0:T(8,128)} copy(f32[4,2,48,128]{3,2,1,0:T(8,128)S(1)} %shard_map.28) | data formatting | bytes 393216
